TPU v7x, 256 devices: a whole 4x4x8 slice. The times are simulated.
256 devices in a mesh: district: 16 (over x, z_hi), tile: 16 (over z_lo, y, core).
Axes of the slice: x: 4, y: 4, z: 8 (z_hi: 4, z_lo: 2; z = z_hi * 2 + z_lo), core: 2. Of those that a mesh axis runs over, the one named last changes fastest.
Arguments:
- parent_state: float32 [3, 256, 2048], P(None, 'district', 'tile'), may hold values from -6 to 6
- parent_depth: float32 [256, 2048], P('district', 'tile'), may hold values from 0.25 to 1
- child_state: float32 [3, 1024, 2048], P(None, 'district', 'tile'), may hold values from -6 to 6
- child_depth: float32 [1024, 2048], P('district', 'tile'), may hold values from 0.1 to 1
- child_wet: int32 [4, 1024, 2048], P(None, 'district', 'tile'), may hold values 0 or 1
- interior_state: float32 [3, 16384, 128], P(None, ('district', 'tile')), may hold values from -6 to 6
- interior_wet: int32 [4, 16384, 128], P(None, ('district', 'tile')), may hold values 0 or 1
- parent_anchor: int32 [16, 16, 2], P('district'), may hold values from 0 to 2044, as said below
- open_row: int32 [16384], P(('district', 'tile')), may hold values from 0 to 63
- open_col: int32 [16384], P(('district', 'tile')), may hold values from 0 to 96
- open_owner: int32 [16384, 1], P(('district', 'tile')), may hold values from 0 to 15; in each aligned block of 64 rows (0 to 63, 64 to 127, ...) at most 8 rows name the same one
- open_valid: int32 [16384], P(('district', 'tile')), may hold values 0 or 1
- open_conduct: float32 [16384], P(('district', 'tile')), may hold values from 0.1 to 0.5
- door_rows: int32 [256, 128], P(('district', 'tile')), may hold values from 0 to 63
Outputs:
- parent_final: float32 [3, 256, 2048], P(None, 'district', 'tile')
- child_final: float32 [3, 1024, 2048], P(None, 'district', 'tile')
- interior_final: float32 [3, 16384, 128], P(None, ('district', 'tile'))
Inputs may be any that keep to these rules, and one draw needn't show every extreme that they name: `open_owner`: tile indices within the opening's own district group; among the rows of one device no owner is named by more than 8 rows, padded ones included. `parent_anchor`: entry 0 is the same for all tiles of a district and leaves room for 2 rows within the district's 16 parent rows; entry 1 rises by 4 from one tile to the next and every window lies within the parent grid's columns; district 0's windows start at column 0 and the last district's end at the grid's last column.
All inputs are finite; a program needn't handle non-finite values. No bound on the sum of `child_wet` or of `interior_wet` or of `open_valid` on one device may be relied on, other than what follows from the above.
Results may differ from a plain program's by a relative error of at most 0.0003.
Values sent between devices are 32-bit elements; how exact they have to be, the bound alone decides.
No kernel may reach another device: no remote copies, remote signals or barrier semaphores. Data moves between devices by JAX's collectives and lax.ppermute only.
A program may use at most 64 MiB of HBM per device.

v0:
```python
import jax
import jax.numpy as jnp
from jax import lax
from jax.sharding import PartitionSpec as P

CX = 64
CY = 128
IY = 128
R = 32
STEPS = 4
CAP = 8
SEG = 32
WX = 2
WY = 4
courant = 0.3
nudging = 0.25
area_ratio = 0.0625


def padded_2(cells, sides, width):
    for axis, dim in sides:
        count = lax.axis_size(axis)
        ends = count - 1
        head = lax.slice_in_dim(cells, 0, width, axis=dim)
        tail = lax.slice_in_dim(cells, cells.shape[dim] - width, cells.shape[dim], axis=dim)
        cells = jnp.concatenate(
            [
                lax.ppermute(tail, axis, [(i, (i + 1) % count) for i in range(ends)]),
                cells,
                lax.ppermute(head, axis, [((i + 1) % count, i) for i in range(ends)]),
            ],
            axis=dim,
        )
    return cells


def advance(padded, wet_cells):
    surface = padded[0]
    east_flow = padded[1]
    north_flow = padded[2]
    wet_depth = padded[3]
    new_east = east_flow[1:-1, 2:-2] - courant * (surface[2:, 2:-2] - surface[:-2, 2:-2])
    new_north = north_flow[2:-2, 1:-1] - courant * (surface[2:-2, 2:] - surface[2:-2, :-2])
    flux_east = wet_depth[1:-1, 2:-2] * new_east
    flux_north = wet_depth[2:-2, 1:-1] * new_north
    new_surface = surface[2:-2, 2:-2] - courant * (
        flux_east[2:] - flux_east[:-2] + flux_north[:, 2:] - flux_north[:, :-2]
    )
    return (new_surface, wet_cells * new_east[1:-1], wet_cells * new_north[:, 1:-1])


def room_step(state, wet_cells):
    padded = jnp.pad(jnp.concatenate([state, wet_cells[None]], 0), ((0, 0), (2, 2), (2, 2)))
    return jnp.stack(advance(padded, wet_cells))


def ranks(owners, tile_count):
    matches = (owners[:, None] == jnp.arange(tile_count, dtype=jnp.int32)[None, :]).astype(
        jnp.int32
    )
    return jnp.sum(jnp.cumsum(matches, 0) * matches, 1) - 1


def place_rows(values, owners, slot_of, tile_count):
    empty = jnp.zeros((tile_count, CAP) + values.shape[1:], values.dtype)
    return empty.at[owners, slot_of].set(values)


def opening_flow(street, weights, face_rows):
    inflow = weights[..., None] * (jnp.repeat(street, 4, axis=-1) - face_rows)
    grouped = inflow.reshape(inflow.shape[:-1] + (inflow.shape[-1] // 4, 4))
    return (inflow, jnp.sum(grouped, -1) * area_ratio)


def absorb(surface, room_rows, street, weights):
    face_rows = surface[room_rows].reshape(weights.shape + (IY,))
    inflow, flux_back = opening_flow(street, weights, face_rows)
    return (surface.at[room_rows].add(inflow.reshape(-1, IY)), flux_back)


def body(
    parent_state,
    parent_depth,
    child_state,
    child_depth,
    child_wet,
    interior_state,
    interior_wet,
    parent_anchor,
    open_row,
    open_col,
    open_owner,
    open_valid,
    open_conduct,
    door_rows,
):
    tile_count = lax.axis_size("tile")
    my_tile = lax.axis_index("tile")
    requests = parent_anchor[0]
    anchor = requests[my_tile]
    owners = open_owner[:, 0]
    slot_of = ranks(owners, tile_count)
    cell_ids = (open_row * CY + open_col)[:, None] + jnp.arange(SEG, dtype=jnp.int32)[None, :]
    weights = place_rows(open_conduct * open_valid.astype(jnp.float32), owners, slot_of, tile_count)
    room_rows = door_rows[0]
    parent_now = parent_state
    child_now = child_state
    rooms_now = interior_state
    for section_index in range(STEPS):
        parent_stack = jnp.concatenate([parent_now, parent_depth[None]], 0)
        padded = padded_2(parent_stack, (("district", 1), ("tile", 2)), 2)
        surface, east_flow, north_flow = advance(padded, 1.0)
        parent_now = jnp.stack([surface, east_flow, north_flow])
        district_rows = lax.all_gather(surface, "tile", axis=1, tiled=True)
        window = lax.dynamic_slice(district_rows, (anchor[0], anchor[1]), (WX, WY))
        target = jnp.broadcast_to(window[:, None, :, None], (WX, R, WY, R)).reshape(CX, CY)
        wet_now = child_wet[section_index].astype(jnp.float32)
        child_stack = jnp.concatenate([child_now, (child_depth * wet_now)[None]], 0)
        padded = padded_2(child_stack, (("district", 1), ("tile", 2)), 2)
        surface, east_flow, north_flow = advance(padded, wet_now)
        surface = surface + nudging * (target - surface)
        rooms_now = room_step(rooms_now, interior_wet[section_index].astype(jnp.float32))
        flat_level = surface.reshape(-1)
        street = place_rows(flat_level[cell_ids], owners, slot_of, tile_count)
        inbound, inweights = (
            lax.all_to_all(
                street.reshape(tile_count, CAP * SEG),
                "tile",
                split_axis=0,
                concat_axis=0,
                tiled=True,
            ),
            lax.all_to_all(weights, "tile", split_axis=0, concat_axis=0, tiled=True),
        )
        inbound = inbound.reshape(tile_count, CAP, SEG)
        room_surface, flux_back = absorb(rooms_now[0], room_rows, inbound, inweights)
        returned = lax.all_to_all(
            flux_back.reshape(tile_count, CAP * SEG),
            "tile",
            split_axis=0,
            concat_axis=0,
            tiled=True,
        )
        returned = returned.reshape(tile_count, CAP, SEG)
        rooms_now = rooms_now.at[0].set(room_surface)
        flat_level = flat_level.at[cell_ids].add(-returned[owners, slot_of])
        child_now = jnp.stack([flat_level.reshape(CX, CY), east_flow, north_flow])
    return (parent_now, child_now, rooms_now)


def solution(mesh):
    return jax.shard_map(
        body,
        mesh=mesh,
        in_specs=(
            P(None, "district", "tile"),
            P("district", "tile"),
            P(None, "district", "tile"),
            P("district", "tile"),
            P(None, "district", "tile"),
            P(None, ("district", "tile"), None),
            P(None, ("district", "tile"), None),
            P("district", None, None),
            P(("district", "tile")),
            P(("district", "tile")),
            P(("district", "tile"), None),
            P(("district", "tile")),
            P(("district", "tile")),
            P(("district", "tile"), None),
        ),
        out_specs=(
            P(None, "district", "tile"),
            P(None, "district", "tile"),
            P(None, ("district", "tile"), None),
        ),
        check_vma=False,
    )
```

profile of v0, /device:TPU:67, one launch (start us, length us, event | category | flops | bytes accessed | tf_op | source)
XLA Modules:
  0.0 467.1 jit_solution(14156101166894164927)
XLA Ops:
  1.4 6.1 %collective-permute-start = (f32[4,2,128]{2,1,0:T(2,128)S(1)}, f32[4,2,128]{2,1,0:T(2,128)S(1)}, u32[]{:S(2)}, u32[]{:S(2)}) collective-permute-start(f32[4,2,128]{2,1,0:T(2,128)S(1)} %get-tuple-element.203), channel_id=1, source_target_pairs={{0,16},{16,32},{32,48},{48,64},{64,80},{80,96},{96,112},{112,128},... | collective-permute-start | bytes 12296 | tf_op jit(solution)/shard_map/ppermute | solution.py:28
  10.4 5.5 %collective-permute-start.16 = (f32[4,2,128]{2,1,0:T(2,128)S(1)}, f32[4,2,128]{2,1,0:T(2,128)S(1)}, u32[]{:S(2)}, u32[]{:S(2)}) collective-permute-start(f32[4,2,128]{2,1,0:T(2,128)S(1)} %get-tuple-element.171), channel_id=1, source_target_pairs={{0,16},{16,32},{32,48},{48,64},{64,80},{80,96},{96,112},{112,128},... | collective-permute-start | bytes 12296 | tf_op jit(solution)/shard_map/ppermute | solution.py:28
  23.1 6.5 %all-to-all-start = ((f32[16,1,8]{2,1,0:T(1,128)}), f32[16,1,8]{2,1,0:T(1,128)S(1)}, u32[]{:S(2)}, u32[]{:S(2)}) async-start(f32[16,1,8]{2,1,0:T(1,128)} %copy.81), calls=%async_computation | async-start | bytes 16384 | tf_op jit(solution)/shard_map/all_to_all | solution.py:133
  39.6 3.5 collective-permute-start.2
  45.2 3.6 collective-permute-start.18
  51.3 20.3 %all_gather.12 = f32[16,2048]{1,0:T(8,128)S(1)} all-gather(f32[16,128]{1,0:T(8,128)S(1)} %fusion.135), channel_id=1, replica_groups=mesh['district'=16,'tile'=16] {'tile'}, dimensions={1}, use_global_device_ids=true | all-gather | bytes 139264 | tf_op jit(solution)/shard_map/all_gather | solution.py:114
  72.0 5.8 %collective-permute-start.4 = (f32[4,2,128]{2,1,0:T(2,128)S(1)}, f32[4,2,128]{2,1,0:T(2,128)S(1)}, u32[]{:S(2)}, u32[]{:S(2)}) collective-permute-start(f32[4,2,128]{2,1,0:T(2,128)S(1)} %get-tuple-element.201), channel_id=1, source_target_pairs={{0,16},{16,32},{32,48},{48,64},{64,80},{80,96},{96,112},{112,128},... | collective-permute-start | bytes 12296 | tf_op jit(solution)/shard_map/ppermute | solution.py:28
  80.0 4.1 collective-permute-done.5
  95.2 4.3 collective-permute-start.9
  99.5 11.8 %gather_fusion = f32[2048]{0:T(1024)S(1)} fusion(f32[8192]{0:T(1024)S(1)} %add_bitcast_fusion.3, s32[2048]{0:T(1024)S(1)} %broadcast_clamp_fusion), kind=kCustom, calls=%fused_computation | custom fusion | bytes 24576 | tf_op jit(solution)/shard_map/gather | solution.py:124
  111.4 3.6 scatter_fusion.1
  115.7 8.8 %all-to-all-start.1 = ((f32[16,1,256]{2,1,0:T(1,128)}), f32[16,1,256]{2,1,0:T(1,128)S(1)}, u32[]{:S(2)}, u32[]{:S(2)}) async-start(f32[16,1,256]{2,1,0:T(1,128)} %all_to_all.51), calls=%async_computation.1 | async-start | bytes 32768 | tf_op jit(solution)/shard_map/all_to_all | solution.py:126
  124.6 3.5 collective-permute-start.10
  140.3 19.2 %all_gather.13 = f32[16,2048]{1,0:T(8,128)S(1)} all-gather(f32[16,128]{1,0:T(8,128)S(1)} %fusion.133), channel_id=1, replica_groups=mesh['district'=16,'tile'=16] {'tile'}, dimensions={1}, use_global_device_ids=true | all-gather | bytes 139264 | tf_op jit(solution)/shard_map/all_gather | solution.py:114
  164.2 17.7 %all_gather.14 = f32[16,2048]{1,0:T(8,128)S(1)} all-gather(f32[16,128]{1,0:T(8,128)S(1)} %fusion.131), channel_id=1, replica_groups=mesh['district'=16,'tile'=16] {'tile'}, dimensions={1}, use_global_device_ids=true | all-gather | bytes 139264 | tf_op jit(solution)/shard_map/all_gather | solution.py:114
  183.3 18.6 %all_gather.15 = f32[16,2048]{1,0:T(8,128)S(1)} all-gather(f32[16,128]{1,0:T(8,128)S(1)} %fusion.129), channel_id=1, replica_groups=mesh['district'=16,'tile'=16] {'tile'}, dimensions={1}, use_global_device_ids=true | all-gather | bytes 139264 | tf_op jit(solution)/shard_map/all_gather | solution.py:114
  206.1 3.5 all-to-all-start.2
  209.7 5.7 %all-to-all-done.2 = f32[16,1,256]{2,1,0:T(1,128)S(1)} async-done(((f32[16,1,256]{2,1,0:T(1,128)}), f32[16,1,256]{2,1,0:T(1,128)S(1)}, u32[]{:S(2)}, u32[]{:S(2)}) %all-to-all-start.2) | async-done | bytes 16416 | tf_op jit(solution)/shard_map/all_to_all | solution.py:137
  216.4 14.7 %scatter_fusion.2 = f32[8192]{0:T(1024)S(1)} fusion(f32[8192]{0:T(1024)S(1)} %add_bitcast_fusion.3, s32[2048]{0:T(1024)S(1)} %reshape.550, f32[2048]{0:T(1024)S(1)} %reshape.552), kind=kCustom, calls=%fused_computation.14 | custom fusion | flops 2048 | bytes 32768 | tf_op jit(solution)/shard_map/scatter-add | solution.py:146
  231.1 4.4 collective-permute-start.20
  238.4 3.6 collective-permute-done.21
  242.1 3.9 collective-permute-start.22
  253.1 11.8 %gather_fusion.3 = f32[2048]{0:T(1024)S(1)} fusion(f32[8192]{0:T(1024)S(1)} %add_bitcast_fusion.2, s32[2048]{0:T(1024)S(1)} %broadcast_clamp_fusion), kind=kCustom, calls=%fused_computation.3 | custom fusion | bytes 24576 | tf_op jit(solution)/shard_map/gather | solution.py:124
  264.9 3.6 scatter_fusion.3
  269.2 6.2 %all-to-all-start.3 = ((f32[16,1,256]{2,1,0:T(1,128)}), f32[16,1,256]{2,1,0:T(1,128)S(1)}, u32[]{:S(2)}, u32[]{:S(2)}) async-start(f32[16,1,256]{2,1,0:T(1,128)} %all_to_all.54), calls=%async_computation.3 | async-start | bytes 32768 | tf_op jit(solution)/shard_map/all_to_all | solution.py:126
  275.5 5.7 %all-to-all-done.3 = f32[16,1,256]{2,1,0:T(1,128)S(1)} async-done(((f32[16,1,256]{2,1,0:T(1,128)}), f32[16,1,256]{2,1,0:T(1,128)S(1)}, u32[]{:S(2)}, u32[]{:S(2)}) %all-to-all-start.3) | async-done | bytes 16416 | tf_op jit(solution)/shard_map/all_to_all | solution.py:126
  285.1 3.7 all-to-all-start.4
  288.8 5.8 %all-to-all-done.4 = f32[16,1,256]{2,1,0:T(1,128)S(1)} async-done(((f32[16,1,256]{2,1,0:T(1,128)}), f32[16,1,256]{2,1,0:T(1,128)S(1)}, u32[]{:S(2)}, u32[]{:S(2)}) %all-to-all-start.4) | async-done | bytes 16416 | tf_op jit(solution)/shard_map/all_to_all | solution.py:137
  295.6 14.5 %scatter_fusion.4 = f32[8192]{0:T(1024)S(1)} fusion(f32[8192]{0:T(1024)S(1)} %add_bitcast_fusion.2, s32[2048]{0:T(1024)S(1)} %reshape.550, f32[2048]{0:T(1024)S(1)} %reshape.574), kind=kCustom, calls=%fused_computation.17 | custom fusion | flops 2048 | bytes 32768 | tf_op jit(solution)/shard_map/scatter-add | solution.py:146
  316.4 4.8 %collective-permute-done.25 = f32[4,2,128]{2,1,0:T(2,128)S(1)} collective-permute-done((f32[4,2,128]{2,1,0:T(2,128)S(1)}, f32[4,2,128]{2,1,0:T(2,128)S(1)}, u32[]{:S(2)}, u32[]{:S(2)}) %collective-permute-start.25) | collective-permute-done | bytes 4128 | tf_op jit(solution)/shard_map/ppermute | solution.py:30
  321.3 3.7 collective-permute-start.26
  332.0 11.8 %gather_fusion.6 = f32[2048]{0:T(1024)S(1)} fusion(f32[8192]{0:T(1024)S(1)} %add_bitcast_fusion.1, s32[2048]{0:T(1024)S(1)} %broadcast_clamp_fusion), kind=kCustom, calls=%fused_computation.6 | custom fusion | bytes 24576 | tf_op jit(solution)/shard_map/gather | solution.py:124
  343.9 3.6 scatter_fusion.5
  348.2 6.2 %all-to-all-start.5 = ((f32[16,1,256]{2,1,0:T(1,128)}), f32[16,1,256]{2,1,0:T(1,128)S(1)}, u32[]{:S(2)}, u32[]{:S(2)}) async-start(f32[16,1,256]{2,1,0:T(1,128)} %all_to_all.57), calls=%async_computation.5 | async-start | bytes 32768 | tf_op jit(solution)/shard_map/all_to_all | solution.py:126
  354.4 5.7 %all-to-all-done.5 = f32[16,1,256]{2,1,0:T(1,128)S(1)} async-done(((f32[16,1,256]{2,1,0:T(1,128)}), f32[16,1,256]{2,1,0:T(1,128)S(1)}, u32[]{:S(2)}, u32[]{:S(2)}) %all-to-all-start.5) | async-done | bytes 16416 | tf_op jit(solution)/shard_map/all_to_all | solution.py:126
  364.0 3.7 all-to-all-start.6
  367.7 5.8 %all-to-all-done.6 = f32[16,1,256]{2,1,0:T(1,128)S(1)} async-done(((f32[16,1,256]{2,1,0:T(1,128)}), f32[16,1,256]{2,1,0:T(1,128)S(1)}, u32[]{:S(2)}, u32[]{:S(2)}) %all-to-all-start.6) | async-done | bytes 16416 | tf_op jit(solution)/shard_map/all_to_all | solution.py:137
  374.5 14.5 %scatter_fusion.6 = f32[8192]{0:T(1024)S(1)} fusion(f32[8192]{0:T(1024)S(1)} %add_bitcast_fusion.1, s32[2048]{0:T(1024)S(1)} %reshape.550, f32[2048]{0:T(1024)S(1)} %reshape.596), kind=kCustom, calls=%fused_computation.20 | custom fusion | flops 2048 | bytes 32768 | tf_op jit(solution)/shard_map/scatter-add | solution.py:146
  389.0 4.6 collective-permute-start.28
  395.6 4.5 collective-permute-done.29
  400.2 3.9 collective-permute-start.30
  411.1 11.8 %gather_fusion.9 = f32[2048]{0:T(1024)S(1)} fusion(f32[8192]{0:T(1024)S(1)} %add_bitcast_fusion, s32[2048]{0:T(1024)S(1)} %broadcast_clamp_fusion), kind=kCustom, calls=%fused_computation.9 | custom fusion | bytes 24576 | tf_op jit(solution)/shard_map/gather | solution.py:124
  423.0 3.6 scatter_fusion.7
  427.3 6.2 %all-to-all-start.7 = ((f32[16,1,256]{2,1,0:T(1,128)}), f32[16,1,256]{2,1,0:T(1,128)S(1)}, u32[]{:S(2)}, u32[]{:S(2)}) async-start(f32[16,1,256]{2,1,0:T(1,128)} %all_to_all.60), calls=%async_computation.7 | async-start | bytes 32768 | tf_op jit(solution)/shard_map/all_to_all | solution.py:126
  433.6 5.7 %all-to-all-done.7 = f32[16,1,256]{2,1,0:T(1,128)S(1)} async-done(((f32[16,1,256]{2,1,0:T(1,128)}), f32[16,1,256]{2,1,0:T(1,128)S(1)}, u32[]{:S(2)}, u32[]{:S(2)}) %all-to-all-start.7) | async-done | bytes 16416 | tf_op jit(solution)/shard_map/all_to_all | solution.py:126
  441.3 3.7 all-to-all-start.8
  446.4 4.5 all-to-all-done.8
  451.8 14.5 %scatter_fusion.8 = f32[8192]{0:T(1024)S(1)} fusion(f32[8192]{0:T(1024)S(1)} %add_bitcast_fusion, s32[2048]{0:T(1024)S(1)} %reshape.550, f32[2048]{0:T(1024)S(1)} %reshape.618), kind=kCustom, calls=%fused_computation.23 | custom fusion | flops 2048 | bytes 32768 | tf_op jit(solution)/shard_map/scatter-add | solution.py:146
  (313 shorter events, 108.2 us)
Async XLA Ops:
  0.6 28.9 %copy-start = (s32[1,16,2]{1,2,0:T(2,128)S(1)}, s32[1,16,2]{1,2,0:T(2,128)}, u32[]{:S(2)}) copy-start(s32[1,16,2]{1,2,0:T(2,128)} %param.29) | copy-start | bytes 388
  0.6 8.9 %copy-start.8 = (f32[64,128]{1,0:T(8,128)S(1)}, f32[64,128]{1,0:T(8,128)}, u32[]{:S(2)}) copy-start(f32[64,128]{1,0:T(8,128)} %param.25) | copy-start | bytes 98308
  1.4 37.5 %collective-permute-start = (f32[4,2,128]{2,1,0:T(2,128)S(1)}, f32[4,2,128]{2,1,0:T(2,128)S(1)}, u32[]{:S(2)}, u32[]{:S(2)}) collective-permute-start(f32[4,2,128]{2,1,0:T(2,128)S(1)} %get-tuple-element.203), channel_id=1, source_target_pairs={{0,16},{16,32},{32,48},{48,64},{64,80},{80,96},{96,112},{112,128},... | collective-permute-start | bytes 12296 | tf_op jit(solution)/shard_map/ppermute | solution.py:28
  7.5 31.4 %collective-permute-start.1 = (f32[4,2,128]{2,1,0:T(2,128)S(1)}, f32[4,2,128]{2,1,0:T(2,128)S(1)}, u32[]{:S(2)}, u32[]{:S(2)}) collective-permute-start(f32[4,2,128]{2,1,0:T(2,128)S(1)} %get-tuple-element.204), channel_id=1, source_target_pairs={{16,0},{32,16},{48,32},{64,48},{80,64},{96,80},{112,96},{128,112},... | collective-permute-start | bytes 12296 | tf_op jit(solution)/shard_map/ppermute | solution.py:30
  10.4 34.6 %collective-permute-start.16 = (f32[4,2,128]{2,1,0:T(2,128)S(1)}, f32[4,2,128]{2,1,0:T(2,128)S(1)}, u32[]{:S(2)}, u32[]{:S(2)}) collective-permute-start(f32[4,2,128]{2,1,0:T(2,128)S(1)} %get-tuple-element.171), channel_id=1, source_target_pairs={{0,16},{16,32},{32,48},{48,64},{64,80},{80,96},{96,112},{112,128},... | collective-permute-start | bytes 12296 | tf_op jit(solution)/shard_map/ppermute | solution.py:28
  15.9 29.2 %collective-permute-start.17 = (f32[4,2,128]{2,1,0:T(2,128)S(1)}, f32[4,2,128]{2,1,0:T(2,128)S(1)}, u32[]{:S(2)}, u32[]{:S(2)}) collective-permute-start(f32[4,2,128]{2,1,0:T(2,128)S(1)} %get-tuple-element.172), channel_id=1, source_target_pairs={{16,0},{32,16},{48,32},{64,48},{80,64},{96,80},{112,96},{128,112},... | collective-permute-start | bytes 12296 | tf_op jit(solution)/shard_map/ppermute | solution.py:30
  18.9 11.2 %copy-start.12 = (s32[64]{0:T(128)S(1)}, s32[64]{0:T(128)}, u32[]{:S(2)}) copy-start(s32[64]{0:T(128)} %param.31) | copy-start | bytes 772
  18.9 11.2 %copy-start.13 = (s32[64]{0:T(128)S(1)}, s32[64]{0:T(128)}, u32[]{:S(2)}) copy-start(s32[64]{0:T(128)} %param.30) | copy-start | bytes 772
  22.4 7.9 %copy-start.3 = (s32[4,64,128]{2,1,0:T(8,128)S(1)}, s32[4,64,128]{2,1,0:T(8,128)}, u32[]{:S(2)}) copy-start(s32[4,64,128]{2,1,0:T(8,128)} %param.28) | copy-start | bytes 393220
  23.1 14.5 %all-to-all-start = ((f32[16,1,8]{2,1,0:T(1,128)}), f32[16,1,8]{2,1,0:T(1,128)S(1)}, u32[]{:S(2)}, u32[]{:S(2)}) async-start(f32[16,1,8]{2,1,0:T(1,128)} %copy.81), calls=%async_computation | async-start | bytes 16384 | tf_op jit(solution)/shard_map/all_to_all | solution.py:133
  39.6 11.2 %collective-permute-start.2 = (f32[4,20,2]{2,1,0:T(8,128)S(1)}, f32[4,20,2]{2,1,0:T(8,128)S(1)}, u32[]{:S(2)}, u32[]{:S(2)}) collective-permute-start(f32[4,20,2]{2,1,0:T(8,128)S(1)} %get-tuple-element.195), channel_id=1, source_target_pairs={{0,1},{1,2},{2,3},{3,4},{4,5},{5,6},{6,7},{7,8},{8,9},{9,10},{10,1... | collective-permute-start | bytes 1928 | tf_op jit(solution)/shard_map/ppermute | solution.py:28
  43.2 7.7 %collective-permute-start.3 = (f32[4,20,2]{2,1,0:T(8,128)S(1)}, f32[4,20,2]{2,1,0:T(8,128)S(1)}, u32[]{:S(2)}, u32[]{:S(2)}) collective-permute-start(f32[4,20,2]{2,1,0:T(8,128)S(1)} %get-tuple-element.196), channel_id=1, source_target_pairs={{1,0},{2,1},{3,2},{4,3},{5,4},{6,5},{7,6},{8,7},{9,8},{10,9},{11,1... | collective-permute-start | bytes 1928 | tf_op jit(solution)/shard_map/ppermute | solution.py:30
  45.2 34.4 %collective-permute-start.18 = (f32[4,68,2]{2,1,0:T(8,128)S(1)}, f32[4,68,2]{2,1,0:T(8,128)S(1)}, u32[]{:S(2)}, u32[]{:S(2)}) collective-permute-start(f32[4,68,2]{2,1,0:T(8,128)S(1)} %get-tuple-element.143), channel_id=1, source_target_pairs={{0,1},{1,2},{2,3},{3,4},{4,5},{5,6},{6,7},{7,8},{8,9},{9,10},{10,1... | collective-permute-start | bytes 6536 | tf_op jit(solution)/shard_map/ppermute | solution.py:28
  48.9 30.8 %collective-permute-start.19 = (f32[4,68,2]{2,1,0:T(8,128)S(1)}, f32[4,68,2]{2,1,0:T(8,128)S(1)}, u32[]{:S(2)}, u32[]{:S(2)}) collective-permute-start(f32[4,68,2]{2,1,0:T(8,128)S(1)} %get-tuple-element.144), channel_id=1, source_target_pairs={{1,0},{2,1},{3,2},{4,3},{5,4},{6,5},{7,6},{8,7},{9,8},{10,9},{11,1... | collective-permute-start | bytes 6536 | tf_op jit(solution)/shard_map/ppermute | solution.py:30
  72.0 8.1 %collective-permute-start.4 = (f32[4,2,128]{2,1,0:T(2,128)S(1)}, f32[4,2,128]{2,1,0:T(2,128)S(1)}, u32[]{:S(2)}, u32[]{:S(2)}) collective-permute-start(f32[4,2,128]{2,1,0:T(2,128)S(1)} %get-tuple-element.201), channel_id=1, source_target_pairs={{0,16},{16,32},{32,48},{48,64},{64,80},{80,96},{96,112},{112,128},... | collective-permute-start | bytes 12296 | tf_op jit(solution)/shard_map/ppermute | solution.py:28
  77.7 6.5 %collective-permute-start.5 = (f32[4,2,128]{2,1,0:T(2,128)S(1)}, f32[4,2,128]{2,1,0:T(2,128)S(1)}, u32[]{:S(2)}, u32[]{:S(2)}) collective-permute-start(f32[4,2,128]{2,1,0:T(2,128)S(1)} %get-tuple-element.202), channel_id=1, source_target_pairs={{16,0},{32,16},{48,32},{64,48},{80,64},{96,80},{112,96},{128,112},... | collective-permute-start | bytes 12296 | tf_op jit(solution)/shard_map/ppermute | solution.py:30
  84.3 5.1 %collective-permute-start.6 = (f32[4,20,2]{2,1,0:T(8,128)S(1)}, f32[4,20,2]{2,1,0:T(8,128)S(1)}, u32[]{:S(2)}, u32[]{:S(2)}) collective-permute-start(f32[4,20,2]{2,1,0:T(8,128)S(1)} %get-tuple-element.193), channel_id=1, source_target_pairs={{0,1},{1,2},{2,3},{3,4},{4,5},{5,6},{6,7},{7,8},{8,9},{9,10},{10,1... | collective-permute-start | bytes 1928 | tf_op jit(solution)/shard_map/ppermute | solution.py:28
  87.3 5.4 %collective-permute-start.7 = (f32[4,20,2]{2,1,0:T(8,128)S(1)}, f32[4,20,2]{2,1,0:T(8,128)S(1)}, u32[]{:S(2)}, u32[]{:S(2)}) collective-permute-start(f32[4,20,2]{2,1,0:T(8,128)S(1)} %get-tuple-element.194), channel_id=1, source_target_pairs={{1,0},{2,1},{3,2},{4,3},{5,4},{6,5},{7,6},{8,7},{9,8},{10,9},{11,1... | collective-permute-start | bytes 1928 | tf_op jit(solution)/shard_map/ppermute | solution.py:30
  93.2 31.3 %collective-permute-start.8 = (f32[4,2,128]{2,1,0:T(2,128)S(1)}, f32[4,2,128]{2,1,0:T(2,128)S(1)}, u32[]{:S(2)}, u32[]{:S(2)}) collective-permute-start(f32[4,2,128]{2,1,0:T(2,128)S(1)} %get-tuple-element.199), channel_id=1, source_target_pairs={{0,16},{16,32},{32,48},{48,64},{64,80},{80,96},{96,112},{112,128},... | collective-permute-start | bytes 12296 | tf_op jit(solution)/shard_map/ppermute | solution.py:28
  95.2 29.4 %collective-permute-start.9 = (f32[4,2,128]{2,1,0:T(2,128)S(1)}, f32[4,2,128]{2,1,0:T(2,128)S(1)}, u32[]{:S(2)}, u32[]{:S(2)}) collective-permute-start(f32[4,2,128]{2,1,0:T(2,128)S(1)} %get-tuple-element.200), channel_id=1, source_target_pairs={{16,0},{32,16},{48,32},{64,48},{80,64},{96,80},{112,96},{128,112},... | collective-permute-start | bytes 12296 | tf_op jit(solution)/shard_map/ppermute | solution.py:30
  115.7 86.6 %all-to-all-start.1 = ((f32[16,1,256]{2,1,0:T(1,128)}), f32[16,1,256]{2,1,0:T(1,128)S(1)}, u32[]{:S(2)}, u32[]{:S(2)}) async-start(f32[16,1,256]{2,1,0:T(1,128)} %all_to_all.51), calls=%async_computation.1 | async-start | bytes 32768 | tf_op jit(solution)/shard_map/all_to_all | solution.py:126
  124.5 5.6 %copy-start.4 = (s32[4,64,128]{2,1,0:T(8,128)S(1)}, s32[4,64,128]{2,1,0:T(8,128)}, u32[]{:S(2)}) copy-start(s32[4,64,128]{2,1,0:T(8,128)} %param.26) | copy-start | bytes 393220
  124.6 5.6 %collective-permute-start.10 = (f32[4,20,2]{2,1,0:T(8,128)S(1)}, f32[4,20,2]{2,1,0:T(8,128)S(1)}, u32[]{:S(2)}, u32[]{:S(2)}) collective-permute-start(f32[4,20,2]{2,1,0:T(8,128)S(1)} %get-tuple-element.191), channel_id=1, source_target_pairs={{0,1},{1,2},{2,3},{3,4},{4,5},{5,6},{6,7},{7,8},{8,9},{9,10},{10,1... | collective-permute-start | bytes 1928 | tf_op jit(solution)/shard_map/ppermute | solution.py:28
  128.2 5.4 %collective-permute-start.11 = (f32[4,20,2]{2,1,0:T(8,128)S(1)}, f32[4,20,2]{2,1,0:T(8,128)S(1)}, u32[]{:S(2)}, u32[]{:S(2)}) collective-permute-start(f32[4,20,2]{2,1,0:T(8,128)S(1)} %get-tuple-element.192), channel_id=1, source_target_pairs={{1,0},{2,1},{3,2},{4,3},{5,4},{6,5},{7,6},{8,7},{9,8},{10,9},{11,1... | collective-permute-start | bytes 1928 | tf_op jit(solution)/shard_map/ppermute | solution.py:30
  134.1 25.6 %collective-permute-start.12 = (f32[4,2,128]{2,1,0:T(2,128)S(1)}, f32[4,2,128]{2,1,0:T(2,128)S(1)}, u32[]{:S(2)}, u32[]{:S(2)}) collective-permute-start(f32[4,2,128]{2,1,0:T(2,128)S(1)} %get-tuple-element.197), channel_id=1, source_target_pairs={{0,16},{16,32},{32,48},{48,64},{64,80},{80,96},{96,112},{112,128},... | collective-permute-start | bytes 12296 | tf_op jit(solution)/shard_map/ppermute | solution.py:28
  137.3 22.5 %collective-permute-start.13 = (f32[4,2,128]{2,1,0:T(2,128)S(1)}, f32[4,2,128]{2,1,0:T(2,128)S(1)}, u32[]{:S(2)}, u32[]{:S(2)}) collective-permute-start(f32[4,2,128]{2,1,0:T(2,128)S(1)} %get-tuple-element.198), channel_id=1, source_target_pairs={{16,0},{32,16},{48,32},{64,48},{80,64},{96,80},{112,96},{128,112},... | collective-permute-start | bytes 12296 | tf_op jit(solution)/shard_map/ppermute | solution.py:30
  159.8 22.4 %collective-permute-start.14 = (f32[4,20,2]{2,1,0:T(8,128)S(1)}, f32[4,20,2]{2,1,0:T(8,128)S(1)}, u32[]{:S(2)}, u32[]{:S(2)}) collective-permute-start(f32[4,20,2]{2,1,0:T(8,128)S(1)} %get-tuple-element.189), channel_id=1, source_target_pairs={{0,1},{1,2},{2,3},{3,4},{4,5},{5,6},{6,7},{7,8},{8,9},{9,10},{10,1... | collective-permute-start | bytes 1928 | tf_op jit(solution)/shard_map/ppermute | solution.py:28
  161.8 20.5 %collective-permute-start.15 = (f32[4,20,2]{2,1,0:T(8,128)S(1)}, f32[4,20,2]{2,1,0:T(8,128)S(1)}, u32[]{:S(2)}, u32[]{:S(2)}) collective-permute-start(f32[4,20,2]{2,1,0:T(8,128)S(1)} %get-tuple-element.190), channel_id=1, source_target_pairs={{1,0},{2,1},{3,2},{4,3},{5,4},{6,5},{7,6},{8,7},{9,8},{10,9},{11,1... | collective-permute-start | bytes 1928 | tf_op jit(solution)/shard_map/ppermute | solution.py:30
  206.1 9.3 %all-to-all-start.2 = ((f32[16,1,256]{2,1,0:T(1,128)}), f32[16,1,256]{2,1,0:T(1,128)S(1)}, u32[]{:S(2)}, u32[]{:S(2)}) async-start(f32[16,1,256]{2,1,0:T(1,128)} %mul.476), calls=%async_computation.2 | async-start | bytes 32768 | tf_op jit(solution)/shard_map/all_to_all | solution.py:137
  231.1 7.3 %collective-permute-start.20 = (f32[4,2,128]{2,1,0:T(2,128)S(1)}, f32[4,2,128]{2,1,0:T(2,128)S(1)}, u32[]{:S(2)}, u32[]{:S(2)}) collective-permute-start(f32[4,2,128]{2,1,0:T(2,128)S(1)} %get-tuple-element.167), channel_id=1, source_target_pairs={{0,16},{16,32},{32,48},{48,64},{64,80},{80,96},{96,112},{112,128},... | collective-permute-start | bytes 12296 | tf_op jit(solution)/shard_map/ppermute | solution.py:28
  235.5 6.5 %collective-permute-start.21 = (f32[4,2,128]{2,1,0:T(2,128)S(1)}, f32[4,2,128]{2,1,0:T(2,128)S(1)}, u32[]{:S(2)}, u32[]{:S(2)}) collective-permute-start(f32[4,2,128]{2,1,0:T(2,128)S(1)} %get-tuple-element.168), channel_id=1, source_target_pairs={{16,0},{32,16},{48,32},{64,48},{80,64},{96,80},{112,96},{128,112},... | collective-permute-start | bytes 12296 | tf_op jit(solution)/shard_map/ppermute | solution.py:30
  242.1 7.2 %collective-permute-start.22 = (f32[4,68,2]{2,1,0:T(8,128)S(1)}, f32[4,68,2]{2,1,0:T(8,128)S(1)}, u32[]{:S(2)}, u32[]{:S(2)}) collective-permute-start(f32[4,68,2]{2,1,0:T(8,128)S(1)} %get-tuple-element.141), channel_id=1, source_target_pairs={{0,1},{1,2},{2,3},{3,4},{4,5},{5,6},{6,7},{7,8},{8,9},{9,10},{10,1... | collective-permute-start | bytes 6536 | tf_op jit(solution)/shard_map/ppermute | solution.py:28
  246.0 6.5 %collective-permute-start.23 = (f32[4,68,2]{2,1,0:T(8,128)S(1)}, f32[4,68,2]{2,1,0:T(8,128)S(1)}, u32[]{:S(2)}, u32[]{:S(2)}) collective-permute-start(f32[4,68,2]{2,1,0:T(8,128)S(1)} %get-tuple-element.142), channel_id=1, source_target_pairs={{1,0},{2,1},{3,2},{4,3},{5,4},{6,5},{7,6},{8,7},{9,8},{10,9},{11,1... | collective-permute-start | bytes 6536 | tf_op jit(solution)/shard_map/ppermute | solution.py:30
  269.2 12.0 %all-to-all-start.3 = ((f32[16,1,256]{2,1,0:T(1,128)}), f32[16,1,256]{2,1,0:T(1,128)S(1)}, u32[]{:S(2)}, u32[]{:S(2)}) async-start(f32[16,1,256]{2,1,0:T(1,128)} %all_to_all.54), calls=%async_computation.3 | async-start | bytes 32768 | tf_op jit(solution)/shard_map/all_to_all | solution.py:126
  285.1 9.5 %all-to-all-start.4 = ((f32[16,1,256]{2,1,0:T(1,128)}), f32[16,1,256]{2,1,0:T(1,128)S(1)}, u32[]{:S(2)}, u32[]{:S(2)}) async-start(f32[16,1,256]{2,1,0:T(1,128)} %mul.477), calls=%async_computation.4 | async-start | bytes 32768 | tf_op jit(solution)/shard_map/all_to_all | solution.py:137
  310.1 6.3 %collective-permute-start.24 = (f32[4,2,128]{2,1,0:T(2,128)S(1)}, f32[4,2,128]{2,1,0:T(2,128)S(1)}, u32[]{:S(2)}, u32[]{:S(2)}) collective-permute-start(f32[4,2,128]{2,1,0:T(2,128)S(1)} %get-tuple-element.161), channel_id=1, source_target_pairs={{0,16},{16,32},{32,48},{48,64},{64,80},{80,96},{96,112},{112,128},... | collective-permute-start | bytes 12296 | tf_op jit(solution)/shard_map/ppermute | solution.py:28
  313.6 7.6 %collective-permute-start.25 = (f32[4,2,128]{2,1,0:T(2,128)S(1)}, f32[4,2,128]{2,1,0:T(2,128)S(1)}, u32[]{:S(2)}, u32[]{:S(2)}) collective-permute-start(f32[4,2,128]{2,1,0:T(2,128)S(1)} %get-tuple-element.162), channel_id=1, source_target_pairs={{16,0},{32,16},{48,32},{64,48},{80,64},{96,80},{112,96},{128,112},... | collective-permute-start | bytes 12296 | tf_op jit(solution)/shard_map/ppermute | solution.py:30
  321.3 6.9 %collective-permute-start.26 = (f32[4,68,2]{2,1,0:T(8,128)S(1)}, f32[4,68,2]{2,1,0:T(8,128)S(1)}, u32[]{:S(2)}, u32[]{:S(2)}) collective-permute-start(f32[4,68,2]{2,1,0:T(8,128)S(1)} %get-tuple-element.139), channel_id=1, source_target_pairs={{0,1},{1,2},{2,3},{3,4},{4,5},{5,6},{6,7},{7,8},{8,9},{9,10},{10,1... | collective-permute-start | bytes 6536 | tf_op jit(solution)/shard_map/ppermute | solution.py:28
  325.0 6.5 %collective-permute-start.27 = (f32[4,68,2]{2,1,0:T(8,128)S(1)}, f32[4,68,2]{2,1,0:T(8,128)S(1)}, u32[]{:S(2)}, u32[]{:S(2)}) collective-permute-start(f32[4,68,2]{2,1,0:T(8,128)S(1)} %get-tuple-element.140), channel_id=1, source_target_pairs={{1,0},{2,1},{3,2},{4,3},{5,4},{6,5},{7,6},{8,7},{9,8},{10,9},{11,1... | collective-permute-start | bytes 6536 | tf_op jit(solution)/shard_map/ppermute | solution.py:30
  348.2 11.9 %all-to-all-start.5 = ((f32[16,1,256]{2,1,0:T(1,128)}), f32[16,1,256]{2,1,0:T(1,128)S(1)}, u32[]{:S(2)}, u32[]{:S(2)}) async-start(f32[16,1,256]{2,1,0:T(1,128)} %all_to_all.57), calls=%async_computation.5 | async-start | bytes 32768 | tf_op jit(solution)/shard_map/all_to_all | solution.py:126
  364.0 9.5 %all-to-all-start.6 = ((f32[16,1,256]{2,1,0:T(1,128)}), f32[16,1,256]{2,1,0:T(1,128)S(1)}, u32[]{:S(2)}, u32[]{:S(2)}) async-start(f32[16,1,256]{2,1,0:T(1,128)} %mul.478), calls=%async_computation.6 | async-start | bytes 32768 | tf_op jit(solution)/shard_map/all_to_all | solution.py:137
  389.0 6.6 %collective-permute-start.28 = (f32[4,2,128]{2,1,0:T(2,128)S(1)}, f32[4,2,128]{2,1,0:T(2,128)S(1)}, u32[]{:S(2)}, u32[]{:S(2)}) collective-permute-start(f32[4,2,128]{2,1,0:T(2,128)S(1)} %get-tuple-element.155), channel_id=1, source_target_pairs={{0,16},{16,32},{32,48},{48,64},{64,80},{80,96},{96,112},{112,128},... | collective-permute-start | bytes 12296 | tf_op jit(solution)/shard_map/ppermute | solution.py:28
  393.6 6.5 %collective-permute-start.29 = (f32[4,2,128]{2,1,0:T(2,128)S(1)}, f32[4,2,128]{2,1,0:T(2,128)S(1)}, u32[]{:S(2)}, u32[]{:S(2)}) collective-permute-start(f32[4,2,128]{2,1,0:T(2,128)S(1)} %get-tuple-element.156), channel_id=1, source_target_pairs={{16,0},{32,16},{48,32},{64,48},{80,64},{96,80},{112,96},{128,112},... | collective-permute-start | bytes 12296 | tf_op jit(solution)/shard_map/ppermute | solution.py:30
  400.2 7.2 %collective-permute-start.30 = (f32[4,68,2]{2,1,0:T(8,128)S(1)}, f32[4,68,2]{2,1,0:T(8,128)S(1)}, u32[]{:S(2)}, u32[]{:S(2)}) collective-permute-start(f32[4,68,2]{2,1,0:T(8,128)S(1)} %get-tuple-element.137), channel_id=1, source_target_pairs={{0,1},{1,2},{2,3},{3,4},{4,5},{5,6},{6,7},{7,8},{8,9},{9,10},{10,1... | collective-permute-start | bytes 6536 | tf_op jit(solution)/shard_map/ppermute | solution.py:28
  404.1 6.5 %collective-permute-start.31 = (f32[4,68,2]{2,1,0:T(8,128)S(1)}, f32[4,68,2]{2,1,0:T(8,128)S(1)}, u32[]{:S(2)}, u32[]{:S(2)}) collective-permute-start(f32[4,68,2]{2,1,0:T(8,128)S(1)} %get-tuple-element.138), channel_id=1, source_target_pairs={{1,0},{2,1},{3,2},{4,3},{5,4},{6,5},{7,6},{8,7},{9,8},{10,9},{11,1... | collective-permute-start | bytes 6536 | tf_op jit(solution)/shard_map/ppermute | solution.py:30
  427.3 12.0 %all-to-all-start.7 = ((f32[16,1,256]{2,1,0:T(1,128)}), f32[16,1,256]{2,1,0:T(1,128)S(1)}, u32[]{:S(2)}, u32[]{:S(2)}) async-start(f32[16,1,256]{2,1,0:T(1,128)} %all_to_all.60), calls=%async_computation.7 | async-start | bytes 32768 | tf_op jit(solution)/shard_map/all_to_all | solution.py:126
  441.3 9.5 %all-to-all-start.8 = ((f32[16,1,256]{2,1,0:T(1,128)}), f32[16,1,256]{2,1,0:T(1,128)S(1)}, u32[]{:S(2)}, u32[]{:S(2)}) async-start(f32[16,1,256]{2,1,0:T(1,128)} %mul.479), calls=%async_computation.8 | async-start | bytes 32768 | tf_op jit(solution)/shard_map/all_to_all | solution.py:137
  446.4 5.4 %copy-start.6 = (f32[3,64,128]{2,1,0:T(8,128)}, f32[3,64,128]{2,1,0:T(8,128)S(1)}, u32[]{:S(2)}) copy-start(f32[3,64,128]{2,1,0:T(8,128)S(1)} %bitcast_dynamic-update-slice_fusion) | copy-start | bytes 294916
  (8 other events, 11.7 us)
where the time goes:
time: 469 us; the launch traced here: 467 us
  starting transfers between devices  147 us (31%)
  local copies, waits for them, and re-layouts  91 us (19%)
  blocking collectives  75.9 us (16%)
  other arithmetic  75 us (16%)
  waiting for transfers between devices  72.2 us (15%)
  between operations  6.22 us (1%)
    all_gather x4, blocking collectives, body(): district_rows = lax.all_gather(surface, 'tile', axis=1, tiled=True)  75.9 us
    ppermute x16, starting transfers between devices, padded_2(): lax.ppermute(tail, axis, [(i, (i + 1) % count) for i in range(ends)])  61.9 us
    scatter-add x4, other arithmetic, body(): flat_level = flat_level.at[cell_ids].add(-returned[owners, slot_of])  58.4 us
    gather x8, local copies, waits for them, and re-layouts, body(): street = place_rows(flat_level[cell_ids], owners, slot_of, tile_count)  47.4 us
    ppermute x16, starting transfers between devices, padded_2(): lax.ppermute(head, axis, [((i + 1) % count, i) for i in range(ends)])  36.4 us
    ppermute x16, waiting for transfers between devices, padded_2(): lax.ppermute(head, axis, [((i + 1) % count, i) for i in range(ends)])  33.3 us
    all_to_all x4, starting transfers between devices, body(): lax.all_to_all(street.reshape(tile_count, CAP * SEG), 'tile', split_axis=...  27.4 us
    all_to_all x4, waiting for transfers between devices, body(): lax.all_to_all(flux_back.reshape(tile_count, CAP * SEG), 'tile', split_ax...  21.7 us
  transfers between devices with their start and end apart: 41, of which 16 were waited for; matrix products, arithmetic and copies ran while one was open for 7% of the time, Pallas kernels for 0%

commit v1 on v0

--- a/solution.py
+++ b/solution.py
@@ -2,6 +2,7 @@
 import jax.numpy as jnp
 from jax import lax
 from jax.sharding import PartitionSpec as P
+from jax.lax import all_to_all, psum
 
 CX = 64
 CY = 128
@@ -111,7 +112,9 @@
         padded = padded_2(parent_stack, (("district", 1), ("tile", 2)), 2)
         surface, east_flow, north_flow = advance(padded, 1.0)
         parent_now = jnp.stack([surface, east_flow, north_flow])
-        district_rows = lax.all_gather(surface, "tile", axis=1, tiled=True)
+        moved = jnp.stack([surface for _ in range(psum(1, "tile"))], axis=0)
+        ready = all_to_all(moved, "tile", 0, 0)
+        district_rows = jnp.concatenate(ready, axis=1)
         window = lax.dynamic_slice(district_rows, (anchor[0], anchor[1]), (WX, WY))
         target = jnp.broadcast_to(window[:, None, :, None], (WX, R, WY, R)).reshape(CX, CY)
         wet_now = child_wet[section_index].astype(jnp.float32)

time: 469 us -> 446 us (0.951)
  blocking collectives: 75.9 us -> 0 us
  waiting for transfers between devices: 72.2 us -> 97.4 us
  starting transfers between devices: 147 us -> 170 us
    all_gather x4 -> x0, blocking collectives: 75.9 us -> none  [body(): district_rows = lax.all_gather(surface, 'tile', axis=1, tiled=True)]
    all_to_all x0 -> x4, starting transfers between devices: none -> 27.6 us  [body(): ready = all_to_all(moved, 'tile', 0, 0)]
    all_to_all x0 -> x4, waiting for transfers between devices: none -> 11.8 us  [body(): ready = all_to_all(moved, 'tile', 0, 0)]
    ppermute x16, waiting for transfers between devices: 33.3 us -> 41.2 us  [padded_2(): lax.ppermute(head, axis, [((i + 1) % count, i) for i in range(ends)])]
    all_to_all x4, waiting for transfers between devices: 17.1 us -> 22.7 us  [body(): lax.all_to_all(street.reshape(tile_count, CAP * SEG), 'tile', split_axis=...]
    all_to_all x4, starting transfers between devices: 27.4 us -> 22.6 us  [body(): lax.all_to_all(street.reshape(tile_count, CAP * SEG), 'tile', split_axis=...]
  transfers between devices with their start and end apart: 41 -> 45, of which waited for: 16 -> 22; matrix products, arithmetic and copies ran while one was open for 7% -> 8% of each run, Pallas kernels for 0% -> 0%
where the time goes in v1:
time: 446 us; the launch traced here: 443 us
  starting transfers between devices  170 us (38%)
  waiting for transfers between devices  97.4 us (22%)
  local copies, waits for them, and re-layouts  93.7 us (21%)
  other arithmetic  75.2 us (17%)
  between operations  6.19 us (1%)
    ppermute x16, starting transfers between devices, padded_2(): lax.ppermute(tail, axis, [(i, (i + 1) % count) for i in range(ends)])  62.6 us
    scatter-add x4, other arithmetic, body(): flat_level = flat_level.at[cell_ids].add(-returned[owners, slot_of])  58.4 us
    gather x8, local copies, waits for them, and re-layouts, body(): street = place_rows(flat_level[cell_ids], owners, slot_of, tile_count)  47.4 us
    ppermute x16, waiting for transfers between devices, padded_2(): lax.ppermute(head, axis, [((i + 1) % count, i) for i in range(ends)])  41.2 us
    ppermute x16, starting transfers between devices, padded_2(): lax.ppermute(head, axis, [((i + 1) % count, i) for i in range(ends)])  36.1 us
    all_to_all x4, starting transfers between devices, body(): ready = all_to_all(moved, 'tile', 0, 0)  27.6 us
    all_to_all x4, waiting for transfers between devices, body(): lax.all_to_all(street.reshape(tile_count, CAP * SEG), 'tile', split_axis=...  22.7 us
    all_to_all x4, starting transfers between devices, body(): lax.all_to_all(street.reshape(tile_count, CAP * SEG), 'tile', split_axis=...  22.6 us
  transfers between devices with their start and end apart: 45, of which 22 were waited for; matrix products, arithmetic and copies ran while one was open for 8% of the time, Pallas kernels for 0%

profile of v1, /device:TPU:67, one launch (start us, length us, event | category | flops | bytes accessed | tf_op | source)
XLA Modules:
  0.0 442.6 jit_solution(2965842821156440974)
XLA Ops:
  1.4 6.1 %collective-permute-start = (f32[4,2,128]{2,1,0:T(2,128)S(1)}, f32[4,2,128]{2,1,0:T(2,128)S(1)}, u32[]{:S(2)}, u32[]{:S(2)}) collective-permute-start(f32[4,2,128]{2,1,0:T(2,128)S(1)} %get-tuple-element.203), channel_id=1, source_target_pairs={{0,16},{16,32},{32,48},{48,64},{64,80},{80,96},{96,112},{112,128},... | collective-permute-start | bytes 12296 | tf_op jit(solution)/shard_map/ppermute | solution.py:29
  10.4 5.5 %collective-permute-start.16 = (f32[4,2,128]{2,1,0:T(2,128)S(1)}, f32[4,2,128]{2,1,0:T(2,128)S(1)}, u32[]{:S(2)}, u32[]{:S(2)}) collective-permute-start(f32[4,2,128]{2,1,0:T(2,128)S(1)} %get-tuple-element.171), channel_id=1, source_target_pairs={{0,16},{16,32},{32,48},{48,64},{64,80},{80,96},{96,112},{112,128},... | collective-permute-start | bytes 12296 | tf_op jit(solution)/shard_map/ppermute | solution.py:29
  23.1 6.5 %all-to-all-start.1 = ((f32[16,1,8]{2,1,0:T(1,128)}), f32[16,1,8]{2,1,0:T(1,128)S(1)}, u32[]{:S(2)}, u32[]{:S(2)}) async-start(f32[16,1,8]{2,1,0:T(1,128)} %copy.86), calls=%async_computation.1 | async-start | bytes 16384 | tf_op jit(solution)/shard_map/all_to_all | solution.py:136
  49.1 5.7 %collective-permute-start.4 = (f32[4,2,128]{2,1,0:T(2,128)S(1)}, f32[4,2,128]{2,1,0:T(2,128)S(1)}, u32[]{:S(2)}, u32[]{:S(2)}) collective-permute-start(f32[4,2,128]{2,1,0:T(2,128)S(1)} %get-tuple-element.201), channel_id=1, source_target_pairs={{0,16},{16,32},{32,48},{48,64},{64,80},{80,96},{96,112},{112,128},... | collective-permute-start | bytes 12296 | tf_op jit(solution)/shard_map/ppermute | solution.py:29
  61.9 7.4 %all-to-all-start = ((f32[16,16,128]{2,1,0:T(8,128)}), f32[16,16,128]{2,1,0:T(8,128)S(1)}, u32[]{:S(2)}, u32[]{:S(2)}) async-start(f32[16,16,128]{2,1,0:T(8,128)} %stack.97), calls=%async_computation | async-start | bytes 262144 | tf_op jit(solution)/shard_map/all_to_all | solution.py:116
  69.4 3.5 collective-permute-start.6
  78.8 5.8 %collective-permute-start.8 = (f32[4,2,128]{2,1,0:T(2,128)S(1)}, f32[4,2,128]{2,1,0:T(2,128)S(1)}, u32[]{:S(2)}, u32[]{:S(2)}) collective-permute-start(f32[4,2,128]{2,1,0:T(2,128)S(1)} %get-tuple-element.199), channel_id=1, source_target_pairs={{0,16},{16,32},{32,48},{48,64},{64,80},{80,96},{96,112},{112,128},... | collective-permute-start | bytes 12296 | tf_op jit(solution)/shard_map/ppermute | solution.py:29
  86.5 4.5 %collective-permute-done.9 = f32[4,2,128]{2,1,0:T(2,128)S(1)} collective-permute-done((f32[4,2,128]{2,1,0:T(2,128)S(1)}, f32[4,2,128]{2,1,0:T(2,128)S(1)}, u32[]{:S(2)}, u32[]{:S(2)}) %collective-permute-start.9) | collective-permute-done | bytes 4128 | tf_op jit(solution)/shard_map/ppermute | solution.py:31
  102.3 4.3 collective-permute-start.13
  120.0 10.5 %all-to-all-start.4 = ((f32[16,16,128]{2,1,0:T(8,128)}), f32[16,16,128]{2,1,0:T(8,128)S(1)}, u32[]{:S(2)}, u32[]{:S(2)}) async-start(f32[16,16,128]{2,1,0:T(8,128)} %stack.100), calls=%async_computation.4 | async-start | bytes 262144 | tf_op jit(solution)/shard_map/all_to_all | solution.py:116
  130.9 11.8 %gather_fusion = f32[2048]{0:T(1024)S(1)} fusion(f32[8192]{0:T(1024)S(1)} %add_bitcast_fusion.3, s32[2048]{0:T(1024)S(1)} %broadcast_clamp_fusion), kind=kCustom, calls=%fused_computation | custom fusion | bytes 24576 | tf_op jit(solution)/shard_map/gather | solution.py:127
  142.8 3.6 scatter_fusion.1
  147.7 5.7 %all-to-all-start.7 = ((f32[16,16,128]{2,1,0:T(8,128)}), f32[16,16,128]{2,1,0:T(8,128)S(1)}, u32[]{:S(2)}, u32[]{:S(2)}) async-start(f32[16,16,128]{2,1,0:T(8,128)} %stack.213), calls=%async_computation.7 | async-start | bytes 262144 | tf_op jit(solution)/shard_map/all_to_all | solution.py:116
  153.8 5.8 %all-to-all-done.7 = f32[16,16,128]{2,1,0:T(8,128)S(1)} async-done(((f32[16,16,128]{2,1,0:T(8,128)}), f32[16,16,128]{2,1,0:T(8,128)S(1)}, u32[]{:S(2)}, u32[]{:S(2)}) %all-to-all-start.7) | async-done | bytes 131104 | tf_op jit(solution)/shard_map/all_to_all | solution.py:116
  160.3 4.0 all-to-all-start.10
  164.5 5.9 %all-to-all-done.10 = f32[16,16,128]{2,1,0:T(8,128)S(1)} async-done(((f32[16,16,128]{2,1,0:T(8,128)}), f32[16,16,128]{2,1,0:T(8,128)S(1)}, u32[]{:S(2)}, u32[]{:S(2)}) %all-to-all-start.10) | async-done | bytes 131104 | tf_op jit(solution)/shard_map/all_to_all | solution.py:116
  170.5 4.0 all-to-all-start.2
  174.7 5.5 %all-to-all-done.2 = f32[16,1,256]{2,1,0:T(1,128)S(1)} async-done(((f32[16,1,256]{2,1,0:T(1,128)}), f32[16,1,256]{2,1,0:T(1,128)S(1)}, u32[]{:S(2)}, u32[]{:S(2)}) %all-to-all-start.2) | async-done | bytes 16416 | tf_op jit(solution)/shard_map/all_to_all | solution.py:129
  184.1 3.7 all-to-all-start.3
  187.9 5.8 %all-to-all-done.3 = f32[16,1,256]{2,1,0:T(1,128)S(1)} async-done(((f32[16,1,256]{2,1,0:T(1,128)}), f32[16,1,256]{2,1,0:T(1,128)S(1)}, u32[]{:S(2)}, u32[]{:S(2)}) %all-to-all-start.3) | async-done | bytes 16416 | tf_op jit(solution)/shard_map/all_to_all | solution.py:140
  194.6 14.7 %scatter_fusion.2 = f32[8192]{0:T(1024)S(1)} fusion(f32[8192]{0:T(1024)S(1)} %add_bitcast_fusion.3, s32[2048]{0:T(1024)S(1)} %reshape.590, f32[2048]{0:T(1024)S(1)} %reshape.592), kind=kCustom, calls=%fused_computation.14 | custom fusion | flops 2048 | bytes 32768 | tf_op jit(solution)/shard_map/scatter-add | solution.py:149
  209.4 4.5 %collective-permute-start.20 = (f32[4,2,128]{2,1,0:T(2,128)S(1)}, f32[4,2,128]{2,1,0:T(2,128)S(1)}, u32[]{:S(2)}, u32[]{:S(2)}) collective-permute-start(f32[4,2,128]{2,1,0:T(2,128)S(1)} %get-tuple-element.167), channel_id=1, source_target_pairs={{0,16},{16,32},{32,48},{48,64},{64,80},{80,96},{96,112},{112,128},... | collective-permute-start | bytes 12296 | tf_op jit(solution)/shard_map/ppermute | solution.py:29
  215.9 4.5 %collective-permute-done.21 = f32[4,2,128]{2,1,0:T(2,128)S(1)} collective-permute-done((f32[4,2,128]{2,1,0:T(2,128)S(1)}, f32[4,2,128]{2,1,0:T(2,128)S(1)}, u32[]{:S(2)}, u32[]{:S(2)}) %collective-permute-start.21) | collective-permute-done | bytes 4128 | tf_op jit(solution)/shard_map/ppermute | solution.py:31
  220.5 3.9 collective-permute-start.22
  231.5 11.8 %gather_fusion.3 = f32[2048]{0:T(1024)S(1)} fusion(f32[8192]{0:T(1024)S(1)} %add_bitcast_fusion.2, s32[2048]{0:T(1024)S(1)} %broadcast_clamp_fusion), kind=kCustom, calls=%fused_computation.3 | custom fusion | bytes 24576 | tf_op jit(solution)/shard_map/gather | solution.py:127
  243.3 3.6 scatter_fusion.3
  247.6 6.2 %all-to-all-start.5 = ((f32[16,1,256]{2,1,0:T(1,128)}), f32[16,1,256]{2,1,0:T(1,128)S(1)}, u32[]{:S(2)}, u32[]{:S(2)}) async-start(f32[16,1,256]{2,1,0:T(1,128)} %all_to_all.68), calls=%async_computation.5 | async-start | bytes 32768 | tf_op jit(solution)/shard_map/all_to_all | solution.py:129
  253.9 5.7 %all-to-all-done.5 = f32[16,1,256]{2,1,0:T(1,128)S(1)} async-done(((f32[16,1,256]{2,1,0:T(1,128)}), f32[16,1,256]{2,1,0:T(1,128)S(1)}, u32[]{:S(2)}, u32[]{:S(2)}) %all-to-all-start.5) | async-done | bytes 16416 | tf_op jit(solution)/shard_map/all_to_all | solution.py:129
  263.4 3.7 all-to-all-start.6
  267.2 5.8 %all-to-all-done.6 = f32[16,1,256]{2,1,0:T(1,128)S(1)} async-done(((f32[16,1,256]{2,1,0:T(1,128)}), f32[16,1,256]{2,1,0:T(1,128)S(1)}, u32[]{:S(2)}, u32[]{:S(2)}) %all-to-all-start.6) | async-done | bytes 16416 | tf_op jit(solution)/shard_map/all_to_all | solution.py:140
  273.9 14.5 %scatter_fusion.4 = f32[8192]{0:T(1024)S(1)} fusion(f32[8192]{0:T(1024)S(1)} %add_bitcast_fusion.2, s32[2048]{0:T(1024)S(1)} %reshape.590, f32[2048]{0:T(1024)S(1)} %reshape.614), kind=kCustom, calls=%fused_computation.17 | custom fusion | flops 2048 | bytes 32768 | tf_op jit(solution)/shard_map/scatter-add | solution.py:149
  291.0 3.7 collective-permute-start.25
  297.7 3.9 collective-permute-start.26
  308.6 11.8 %gather_fusion.6 = f32[2048]{0:T(1024)S(1)} fusion(f32[8192]{0:T(1024)S(1)} %add_bitcast_fusion.1, s32[2048]{0:T(1024)S(1)} %broadcast_clamp_fusion), kind=kCustom, calls=%fused_computation.6 | custom fusion | bytes 24576 | tf_op jit(solution)/shard_map/gather | solution.py:127
  320.5 3.6 scatter_fusion.5
  324.7 6.2 %all-to-all-start.8 = ((f32[16,1,256]{2,1,0:T(1,128)}), f32[16,1,256]{2,1,0:T(1,128)S(1)}, u32[]{:S(2)}, u32[]{:S(2)}) async-start(f32[16,1,256]{2,1,0:T(1,128)} %all_to_all.72), calls=%async_computation.8 | async-start | bytes 32768 | tf_op jit(solution)/shard_map/all_to_all | solution.py:129
  331.0 5.7 %all-to-all-done.8 = f32[16,1,256]{2,1,0:T(1,128)S(1)} async-done(((f32[16,1,256]{2,1,0:T(1,128)}), f32[16,1,256]{2,1,0:T(1,128)S(1)}, u32[]{:S(2)}, u32[]{:S(2)}) %all-to-all-start.8) | async-done | bytes 16416 | tf_op jit(solution)/shard_map/all_to_all | solution.py:129
  340.8 3.7 all-to-all-start.9
  344.6 5.8 %all-to-all-done.9 = f32[16,1,256]{2,1,0:T(1,128)S(1)} async-done(((f32[16,1,256]{2,1,0:T(1,128)}), f32[16,1,256]{2,1,0:T(1,128)S(1)}, u32[]{:S(2)}, u32[]{:S(2)}) %all-to-all-start.9) | async-done | bytes 16416 | tf_op jit(solution)/shard_map/all_to_all | solution.py:140
  351.3 14.5 %scatter_fusion.6 = f32[8192]{0:T(1024)S(1)} fusion(f32[8192]{0:T(1024)S(1)} %add_bitcast_fusion.1, s32[2048]{0:T(1024)S(1)} %reshape.590, f32[2048]{0:T(1024)S(1)} %reshape.636), kind=kCustom, calls=%fused_computation.20 | custom fusion | flops 2048 | bytes 32768 | tf_op jit(solution)/shard_map/scatter-add | solution.py:149
  375.8 3.9 collective-permute-start.30
  386.7 11.8 %gather_fusion.9 = f32[2048]{0:T(1024)S(1)} fusion(f32[8192]{0:T(1024)S(1)} %add_bitcast_fusion, s32[2048]{0:T(1024)S(1)} %broadcast_clamp_fusion), kind=kCustom, calls=%fused_computation.9 | custom fusion | bytes 24576 | tf_op jit(solution)/shard_map/gather | solution.py:127
  398.6 3.6 scatter_fusion.7
  402.9 6.2 %all-to-all-start.11 = ((f32[16,1,256]{2,1,0:T(1,128)}), f32[16,1,256]{2,1,0:T(1,128)S(1)}, u32[]{:S(2)}, u32[]{:S(2)}) async-start(f32[16,1,256]{2,1,0:T(1,128)} %all_to_all.76), calls=%async_computation.11 | async-start | bytes 32768 | tf_op jit(solution)/shard_map/all_to_all | solution.py:129
  409.2 5.7 %all-to-all-done.11 = f32[16,1,256]{2,1,0:T(1,128)S(1)} async-done(((f32[16,1,256]{2,1,0:T(1,128)}), f32[16,1,256]{2,1,0:T(1,128)S(1)}, u32[]{:S(2)}, u32[]{:S(2)}) %all-to-all-start.11) | async-done | bytes 16416 | tf_op jit(solution)/shard_map/all_to_all | solution.py:129
  416.9 3.7 all-to-all-start.12
  422.0 4.5 %all-to-all-done.12 = f32[16,1,256]{2,1,0:T(1,128)S(1)} async-done(((f32[16,1,256]{2,1,0:T(1,128)}), f32[16,1,256]{2,1,0:T(1,128)S(1)}, u32[]{:S(2)}, u32[]{:S(2)}) %all-to-all-start.12) | async-done | bytes 16416 | tf_op jit(solution)/shard_map/all_to_all | solution.py:140
  427.4 14.5 %scatter_fusion.8 = f32[8192]{0:T(1024)S(1)} fusion(f32[8192]{0:T(1024)S(1)} %add_bitcast_fusion, s32[2048]{0:T(1024)S(1)} %reshape.590, f32[2048]{0:T(1024)S(1)} %reshape.658), kind=kCustom, calls=%fused_computation.23 | custom fusion | flops 2048 | bytes 32768 | tf_op jit(solution)/shard_map/scatter-add | solution.py:149
  (325 shorter events, 129.4 us)
Async XLA Ops:
  0.6 28.9 %copy-start = (s32[1,16,2]{1,2,0:T(2,128)S(1)}, s32[1,16,2]{1,2,0:T(2,128)}, u32[]{:S(2)}) copy-start(s32[1,16,2]{1,2,0:T(2,128)} %param.29) | copy-start | bytes 388
  1.4 37.5 %collective-permute-start = (f32[4,2,128]{2,1,0:T(2,128)S(1)}, f32[4,2,128]{2,1,0:T(2,128)S(1)}, u32[]{:S(2)}, u32[]{:S(2)}) collective-permute-start(f32[4,2,128]{2,1,0:T(2,128)S(1)} %get-tuple-element.203), channel_id=1, source_target_pairs={{0,16},{16,32},{32,48},{48,64},{64,80},{80,96},{96,112},{112,128},... | collective-permute-start | bytes 12296 | tf_op jit(solution)/shard_map/ppermute | solution.py:29
  7.5 31.4 %collective-permute-start.1 = (f32[4,2,128]{2,1,0:T(2,128)S(1)}, f32[4,2,128]{2,1,0:T(2,128)S(1)}, u32[]{:S(2)}, u32[]{:S(2)}) collective-permute-start(f32[4,2,128]{2,1,0:T(2,128)S(1)} %get-tuple-element.204), channel_id=1, source_target_pairs={{16,0},{32,16},{48,32},{64,48},{80,64},{96,80},{112,96},{128,112},... | collective-permute-start | bytes 12296 | tf_op jit(solution)/shard_map/ppermute | solution.py:31
  10.4 34.6 %collective-permute-start.16 = (f32[4,2,128]{2,1,0:T(2,128)S(1)}, f32[4,2,128]{2,1,0:T(2,128)S(1)}, u32[]{:S(2)}, u32[]{:S(2)}) collective-permute-start(f32[4,2,128]{2,1,0:T(2,128)S(1)} %get-tuple-element.171), channel_id=1, source_target_pairs={{0,16},{16,32},{32,48},{48,64},{64,80},{80,96},{96,112},{112,128},... | collective-permute-start | bytes 12296 | tf_op jit(solution)/shard_map/ppermute | solution.py:29
  15.9 29.2 %collective-permute-start.17 = (f32[4,2,128]{2,1,0:T(2,128)S(1)}, f32[4,2,128]{2,1,0:T(2,128)S(1)}, u32[]{:S(2)}, u32[]{:S(2)}) collective-permute-start(f32[4,2,128]{2,1,0:T(2,128)S(1)} %get-tuple-element.172), channel_id=1, source_target_pairs={{16,0},{32,16},{48,32},{64,48},{80,64},{96,80},{112,96},{128,112},... | collective-permute-start | bytes 12296 | tf_op jit(solution)/shard_map/ppermute | solution.py:31
  18.9 11.2 %copy-start.12 = (s32[64]{0:T(128)S(1)}, s32[64]{0:T(128)}, u32[]{:S(2)}) copy-start(s32[64]{0:T(128)} %param.31) | copy-start | bytes 772
  18.9 11.2 %copy-start.13 = (s32[64]{0:T(128)S(1)}, s32[64]{0:T(128)}, u32[]{:S(2)}) copy-start(s32[64]{0:T(128)} %param.30) | copy-start | bytes 772
  23.1 14.5 %all-to-all-start.1 = ((f32[16,1,8]{2,1,0:T(1,128)}), f32[16,1,8]{2,1,0:T(1,128)S(1)}, u32[]{:S(2)}, u32[]{:S(2)}) async-start(f32[16,1,8]{2,1,0:T(1,128)} %copy.86), calls=%async_computation.1 | async-start | bytes 16384 | tf_op jit(solution)/shard_map/all_to_all | solution.py:136
  39.6 5.5 %collective-permute-start.2 = (f32[4,20,2]{2,1,0:T(8,128)S(1)}, f32[4,20,2]{2,1,0:T(8,128)S(1)}, u32[]{:S(2)}, u32[]{:S(2)}) collective-permute-start(f32[4,20,2]{2,1,0:T(8,128)S(1)} %get-tuple-element.195), channel_id=1, source_target_pairs={{0,1},{1,2},{2,3},{3,4},{4,5},{5,6},{6,7},{7,8},{8,9},{9,10},{10,1... | collective-permute-start | bytes 1928 | tf_op jit(solution)/shard_map/ppermute | solution.py:29
  43.2 5.4 %collective-permute-start.3 = (f32[4,20,2]{2,1,0:T(8,128)S(1)}, f32[4,20,2]{2,1,0:T(8,128)S(1)}, u32[]{:S(2)}, u32[]{:S(2)}) collective-permute-start(f32[4,20,2]{2,1,0:T(8,128)S(1)} %get-tuple-element.196), channel_id=1, source_target_pairs={{1,0},{2,1},{3,2},{4,3},{5,4},{6,5},{7,6},{8,7},{9,8},{10,9},{11,1... | collective-permute-start | bytes 1928 | tf_op jit(solution)/shard_map/ppermute | solution.py:31
  49.1 20.2 %collective-permute-start.4 = (f32[4,2,128]{2,1,0:T(2,128)S(1)}, f32[4,2,128]{2,1,0:T(2,128)S(1)}, u32[]{:S(2)}, u32[]{:S(2)}) collective-permute-start(f32[4,2,128]{2,1,0:T(2,128)S(1)} %get-tuple-element.201), channel_id=1, source_target_pairs={{0,16},{16,32},{32,48},{48,64},{64,80},{80,96},{96,112},{112,128},... | collective-permute-start | bytes 12296 | tf_op jit(solution)/shard_map/ppermute | solution.py:29
  54.8 14.5 %collective-permute-start.5 = (f32[4,2,128]{2,1,0:T(2,128)S(1)}, f32[4,2,128]{2,1,0:T(2,128)S(1)}, u32[]{:S(2)}, u32[]{:S(2)}) collective-permute-start(f32[4,2,128]{2,1,0:T(2,128)S(1)} %get-tuple-element.202), channel_id=1, source_target_pairs={{16,0},{32,16},{48,32},{64,48},{80,64},{96,80},{112,96},{128,112},... | collective-permute-start | bytes 12296 | tf_op jit(solution)/shard_map/ppermute | solution.py:31
  56.8 18.0 %collective-permute-start.18 = (f32[4,68,2]{2,1,0:T(8,128)S(1)}, f32[4,68,2]{2,1,0:T(8,128)S(1)}, u32[]{:S(2)}, u32[]{:S(2)}) collective-permute-start(f32[4,68,2]{2,1,0:T(8,128)S(1)} %get-tuple-element.143), channel_id=1, source_target_pairs={{0,1},{1,2},{2,3},{3,4},{4,5},{5,6},{6,7},{7,8},{8,9},{9,10},{10,1... | collective-permute-start | bytes 6536 | tf_op jit(solution)/shard_map/ppermute | solution.py:29
  59.0 15.8 %collective-permute-start.19 = (f32[4,68,2]{2,1,0:T(8,128)S(1)}, f32[4,68,2]{2,1,0:T(8,128)S(1)}, u32[]{:S(2)}, u32[]{:S(2)}) collective-permute-start(f32[4,68,2]{2,1,0:T(8,128)S(1)} %get-tuple-element.144), channel_id=1, source_target_pairs={{1,0},{2,1},{3,2},{4,3},{5,4},{6,5},{7,6},{8,7},{9,8},{10,9},{11,1... | collective-permute-start | bytes 6536 | tf_op jit(solution)/shard_map/ppermute | solution.py:31
  61.9 57.5 %all-to-all-start = ((f32[16,16,128]{2,1,0:T(8,128)}), f32[16,16,128]{2,1,0:T(8,128)S(1)}, u32[]{:S(2)}, u32[]{:S(2)}) async-start(f32[16,16,128]{2,1,0:T(8,128)} %stack.97), calls=%async_computation | async-start | bytes 262144 | tf_op jit(solution)/shard_map/all_to_all | solution.py:116
  69.4 5.7 %collective-permute-start.6 = (f32[4,20,2]{2,1,0:T(8,128)S(1)}, f32[4,20,2]{2,1,0:T(8,128)S(1)}, u32[]{:S(2)}, u32[]{:S(2)}) collective-permute-start(f32[4,20,2]{2,1,0:T(8,128)S(1)} %get-tuple-element.193), channel_id=1, source_target_pairs={{0,1},{1,2},{2,3},{3,4},{4,5},{5,6},{6,7},{7,8},{8,9},{9,10},{10,1... | collective-permute-start | bytes 1928 | tf_op jit(solution)/shard_map/ppermute | solution.py:29
  72.9 5.4 %collective-permute-start.7 = (f32[4,20,2]{2,1,0:T(8,128)S(1)}, f32[4,20,2]{2,1,0:T(8,128)S(1)}, u32[]{:S(2)}, u32[]{:S(2)}) collective-permute-start(f32[4,20,2]{2,1,0:T(8,128)S(1)} %get-tuple-element.194), channel_id=1, source_target_pairs={{1,0},{2,1},{3,2},{4,3},{5,4},{6,5},{7,6},{8,7},{9,8},{10,9},{11,1... | collective-permute-start | bytes 1928 | tf_op jit(solution)/shard_map/ppermute | solution.py:31
  78.8 7.7 %collective-permute-start.8 = (f32[4,2,128]{2,1,0:T(2,128)S(1)}, f32[4,2,128]{2,1,0:T(2,128)S(1)}, u32[]{:S(2)}, u32[]{:S(2)}) collective-permute-start(f32[4,2,128]{2,1,0:T(2,128)S(1)} %get-tuple-element.199), channel_id=1, source_target_pairs={{0,16},{16,32},{32,48},{48,64},{64,80},{80,96},{96,112},{112,128},... | collective-permute-start | bytes 12296 | tf_op jit(solution)/shard_map/ppermute | solution.py:29
  84.6 6.5 %collective-permute-start.9 = (f32[4,2,128]{2,1,0:T(2,128)S(1)}, f32[4,2,128]{2,1,0:T(2,128)S(1)}, u32[]{:S(2)}, u32[]{:S(2)}) collective-permute-start(f32[4,2,128]{2,1,0:T(2,128)S(1)} %get-tuple-element.200), channel_id=1, source_target_pairs={{16,0},{32,16},{48,32},{64,48},{80,64},{96,80},{112,96},{128,112},... | collective-permute-start | bytes 12296 | tf_op jit(solution)/shard_map/ppermute | solution.py:31
  91.1 5.4 %collective-permute-start.10 = (f32[4,20,2]{2,1,0:T(8,128)S(1)}, f32[4,20,2]{2,1,0:T(8,128)S(1)}, u32[]{:S(2)}, u32[]{:S(2)}) collective-permute-start(f32[4,20,2]{2,1,0:T(8,128)S(1)} %get-tuple-element.191), channel_id=1, source_target_pairs={{0,1},{1,2},{2,3},{3,4},{4,5},{5,6},{6,7},{7,8},{8,9},{9,10},{10,1... | collective-permute-start | bytes 1928 | tf_op jit(solution)/shard_map/ppermute | solution.py:29
  94.5 5.4 %collective-permute-start.11 = (f32[4,20,2]{2,1,0:T(8,128)S(1)}, f32[4,20,2]{2,1,0:T(8,128)S(1)}, u32[]{:S(2)}, u32[]{:S(2)}) collective-permute-start(f32[4,20,2]{2,1,0:T(8,128)S(1)} %get-tuple-element.192), channel_id=1, source_target_pairs={{1,0},{2,1},{3,2},{4,3},{5,4},{6,5},{7,6},{8,7},{9,8},{10,9},{11,1... | collective-permute-start | bytes 1928 | tf_op jit(solution)/shard_map/ppermute | solution.py:31
  100.4 6.3 %collective-permute-start.12 = (f32[4,2,128]{2,1,0:T(2,128)S(1)}, f32[4,2,128]{2,1,0:T(2,128)S(1)}, u32[]{:S(2)}, u32[]{:S(2)}) collective-permute-start(f32[4,2,128]{2,1,0:T(2,128)S(1)} %get-tuple-element.197), channel_id=1, source_target_pairs={{0,16},{16,32},{32,48},{48,64},{64,80},{80,96},{96,112},{112,128},... | collective-permute-start | bytes 12296 | tf_op jit(solution)/shard_map/ppermute | solution.py:29
  102.3 7.4 %collective-permute-start.13 = (f32[4,2,128]{2,1,0:T(2,128)S(1)}, f32[4,2,128]{2,1,0:T(2,128)S(1)}, u32[]{:S(2)}, u32[]{:S(2)}) collective-permute-start(f32[4,2,128]{2,1,0:T(2,128)S(1)} %get-tuple-element.198), channel_id=1, source_target_pairs={{16,0},{32,16},{48,32},{64,48},{80,64},{96,80},{112,96},{128,112},... | collective-permute-start | bytes 12296 | tf_op jit(solution)/shard_map/ppermute | solution.py:31
  109.8 5.1 %collective-permute-start.14 = (f32[4,20,2]{2,1,0:T(8,128)S(1)}, f32[4,20,2]{2,1,0:T(8,128)S(1)}, u32[]{:S(2)}, u32[]{:S(2)}) collective-permute-start(f32[4,20,2]{2,1,0:T(8,128)S(1)} %get-tuple-element.189), channel_id=1, source_target_pairs={{0,1},{1,2},{2,3},{3,4},{4,5},{5,6},{6,7},{7,8},{8,9},{9,10},{10,1... | collective-permute-start | bytes 1928 | tf_op jit(solution)/shard_map/ppermute | solution.py:29
  112.8 5.4 %collective-permute-start.15 = (f32[4,20,2]{2,1,0:T(8,128)S(1)}, f32[4,20,2]{2,1,0:T(8,128)S(1)}, u32[]{:S(2)}, u32[]{:S(2)}) collective-permute-start(f32[4,20,2]{2,1,0:T(8,128)S(1)} %get-tuple-element.190), channel_id=1, source_target_pairs={{1,0},{2,1},{3,2},{4,3},{5,4},{6,5},{7,6},{8,7},{9,8},{10,9},{11,1... | collective-permute-start | bytes 1928 | tf_op jit(solution)/shard_map/ppermute | solution.py:31
  120.0 27.1 %all-to-all-start.4 = ((f32[16,16,128]{2,1,0:T(8,128)}), f32[16,16,128]{2,1,0:T(8,128)S(1)}, u32[]{:S(2)}, u32[]{:S(2)}) async-start(f32[16,16,128]{2,1,0:T(8,128)} %stack.100), calls=%async_computation.4 | async-start | bytes 262144 | tf_op jit(solution)/shard_map/all_to_all | solution.py:116
  147.7 11.9 %all-to-all-start.7 = ((f32[16,16,128]{2,1,0:T(8,128)}), f32[16,16,128]{2,1,0:T(8,128)S(1)}, u32[]{:S(2)}, u32[]{:S(2)}) async-start(f32[16,16,128]{2,1,0:T(8,128)} %stack.213), calls=%async_computation.7 | async-start | bytes 262144 | tf_op jit(solution)/shard_map/all_to_all | solution.py:116
  160.3 10.2 %all-to-all-start.10 = ((f32[16,16,128]{2,1,0:T(8,128)}), f32[16,16,128]{2,1,0:T(8,128)S(1)}, u32[]{:S(2)}, u32[]{:S(2)}) async-start(f32[16,16,128]{2,1,0:T(8,128)} %stack.220), calls=%async_computation.10 | async-start | bytes 262144 | tf_op jit(solution)/shard_map/all_to_all | solution.py:116
  170.5 9.8 %all-to-all-start.2 = ((f32[16,1,256]{2,1,0:T(1,128)}), f32[16,1,256]{2,1,0:T(1,128)S(1)}, u32[]{:S(2)}, u32[]{:S(2)}) async-start(f32[16,1,256]{2,1,0:T(1,128)} %all_to_all.64), calls=%async_computation.2 | async-start | bytes 32768 | tf_op jit(solution)/shard_map/all_to_all | solution.py:129
  184.1 9.5 %all-to-all-start.3 = ((f32[16,1,256]{2,1,0:T(1,128)}), f32[16,1,256]{2,1,0:T(1,128)S(1)}, u32[]{:S(2)}, u32[]{:S(2)}) async-start(f32[16,1,256]{2,1,0:T(1,128)} %mul.476), calls=%async_computation.3 | async-start | bytes 32768 | tf_op jit(solution)/shard_map/all_to_all | solution.py:140
  209.4 6.6 %collective-permute-start.20 = (f32[4,2,128]{2,1,0:T(2,128)S(1)}, f32[4,2,128]{2,1,0:T(2,128)S(1)}, u32[]{:S(2)}, u32[]{:S(2)}) collective-permute-start(f32[4,2,128]{2,1,0:T(2,128)S(1)} %get-tuple-element.167), channel_id=1, source_target_pairs={{0,16},{16,32},{32,48},{48,64},{64,80},{80,96},{96,112},{112,128},... | collective-permute-start | bytes 12296 | tf_op jit(solution)/shard_map/ppermute | solution.py:29
  213.9 6.5 %collective-permute-start.21 = (f32[4,2,128]{2,1,0:T(2,128)S(1)}, f32[4,2,128]{2,1,0:T(2,128)S(1)}, u32[]{:S(2)}, u32[]{:S(2)}) collective-permute-start(f32[4,2,128]{2,1,0:T(2,128)S(1)} %get-tuple-element.168), channel_id=1, source_target_pairs={{16,0},{32,16},{48,32},{64,48},{80,64},{96,80},{112,96},{128,112},... | collective-permute-start | bytes 12296 | tf_op jit(solution)/shard_map/ppermute | solution.py:31
  220.5 7.2 %collective-permute-start.22 = (f32[4,68,2]{2,1,0:T(8,128)S(1)}, f32[4,68,2]{2,1,0:T(8,128)S(1)}, u32[]{:S(2)}, u32[]{:S(2)}) collective-permute-start(f32[4,68,2]{2,1,0:T(8,128)S(1)} %get-tuple-element.141), channel_id=1, source_target_pairs={{0,1},{1,2},{2,3},{3,4},{4,5},{5,6},{6,7},{7,8},{8,9},{9,10},{10,1... | collective-permute-start | bytes 6536 | tf_op jit(solution)/shard_map/ppermute | solution.py:29
  224.4 6.5 %collective-permute-start.23 = (f32[4,68,2]{2,1,0:T(8,128)S(1)}, f32[4,68,2]{2,1,0:T(8,128)S(1)}, u32[]{:S(2)}, u32[]{:S(2)}) collective-permute-start(f32[4,68,2]{2,1,0:T(8,128)S(1)} %get-tuple-element.142), channel_id=1, source_target_pairs={{1,0},{2,1},{3,2},{4,3},{5,4},{6,5},{7,6},{8,7},{9,8},{10,9},{11,1... | collective-permute-start | bytes 6536 | tf_op jit(solution)/shard_map/ppermute | solution.py:31
  247.6 12.0 %all-to-all-start.5 = ((f32[16,1,256]{2,1,0:T(1,128)}), f32[16,1,256]{2,1,0:T(1,128)S(1)}, u32[]{:S(2)}, u32[]{:S(2)}) async-start(f32[16,1,256]{2,1,0:T(1,128)} %all_to_all.68), calls=%async_computation.5 | async-start | bytes 32768 | tf_op jit(solution)/shard_map/all_to_all | solution.py:129
  263.4 9.5 %all-to-all-start.6 = ((f32[16,1,256]{2,1,0:T(1,128)}), f32[16,1,256]{2,1,0:T(1,128)S(1)}, u32[]{:S(2)}, u32[]{:S(2)}) async-start(f32[16,1,256]{2,1,0:T(1,128)} %mul.477), calls=%async_computation.6 | async-start | bytes 32768 | tf_op jit(solution)/shard_map/all_to_all | solution.py:140
  288.5 6.3 %collective-permute-start.24 = (f32[4,2,128]{2,1,0:T(2,128)S(1)}, f32[4,2,128]{2,1,0:T(2,128)S(1)}, u32[]{:S(2)}, u32[]{:S(2)}) collective-permute-start(f32[4,2,128]{2,1,0:T(2,128)S(1)} %get-tuple-element.161), channel_id=1, source_target_pairs={{0,16},{16,32},{32,48},{48,64},{64,80},{80,96},{96,112},{112,128},... | collective-permute-start | bytes 12296 | tf_op jit(solution)/shard_map/ppermute | solution.py:29
  291.0 6.5 %collective-permute-start.25 = (f32[4,2,128]{2,1,0:T(2,128)S(1)}, f32[4,2,128]{2,1,0:T(2,128)S(1)}, u32[]{:S(2)}, u32[]{:S(2)}) collective-permute-start(f32[4,2,128]{2,1,0:T(2,128)S(1)} %get-tuple-element.162), channel_id=1, source_target_pairs={{16,0},{32,16},{48,32},{64,48},{80,64},{96,80},{112,96},{128,112},... | collective-permute-start | bytes 12296 | tf_op jit(solution)/shard_map/ppermute | solution.py:31
  297.7 7.2 %collective-permute-start.26 = (f32[4,68,2]{2,1,0:T(8,128)S(1)}, f32[4,68,2]{2,1,0:T(8,128)S(1)}, u32[]{:S(2)}, u32[]{:S(2)}) collective-permute-start(f32[4,68,2]{2,1,0:T(8,128)S(1)} %get-tuple-element.139), channel_id=1, source_target_pairs={{0,1},{1,2},{2,3},{3,4},{4,5},{5,6},{6,7},{7,8},{8,9},{9,10},{10,1... | collective-permute-start | bytes 6536 | tf_op jit(solution)/shard_map/ppermute | solution.py:29
  301.5 6.5 %collective-permute-start.27 = (f32[4,68,2]{2,1,0:T(8,128)S(1)}, f32[4,68,2]{2,1,0:T(8,128)S(1)}, u32[]{:S(2)}, u32[]{:S(2)}) collective-permute-start(f32[4,68,2]{2,1,0:T(8,128)S(1)} %get-tuple-element.140), channel_id=1, source_target_pairs={{1,0},{2,1},{3,2},{4,3},{5,4},{6,5},{7,6},{8,7},{9,8},{10,9},{11,1... | collective-permute-start | bytes 6536 | tf_op jit(solution)/shard_map/ppermute | solution.py:31
  324.7 12.0 %all-to-all-start.8 = ((f32[16,1,256]{2,1,0:T(1,128)}), f32[16,1,256]{2,1,0:T(1,128)S(1)}, u32[]{:S(2)}, u32[]{:S(2)}) async-start(f32[16,1,256]{2,1,0:T(1,128)} %all_to_all.72), calls=%async_computation.8 | async-start | bytes 32768 | tf_op jit(solution)/shard_map/all_to_all | solution.py:129
  340.8 9.5 %all-to-all-start.9 = ((f32[16,1,256]{2,1,0:T(1,128)}), f32[16,1,256]{2,1,0:T(1,128)S(1)}, u32[]{:S(2)}, u32[]{:S(2)}) async-start(f32[16,1,256]{2,1,0:T(1,128)} %mul.478), calls=%async_computation.9 | async-start | bytes 32768 | tf_op jit(solution)/shard_map/all_to_all | solution.py:140
  365.9 6.3 %collective-permute-start.28 = (f32[4,2,128]{2,1,0:T(2,128)S(1)}, f32[4,2,128]{2,1,0:T(2,128)S(1)}, u32[]{:S(2)}, u32[]{:S(2)}) collective-permute-start(f32[4,2,128]{2,1,0:T(2,128)S(1)} %get-tuple-element.155), channel_id=1, source_target_pairs={{0,16},{16,32},{32,48},{48,64},{64,80},{80,96},{96,112},{112,128},... | collective-permute-start | bytes 12296 | tf_op jit(solution)/shard_map/ppermute | solution.py:29
  369.2 6.5 %collective-permute-start.29 = (f32[4,2,128]{2,1,0:T(2,128)S(1)}, f32[4,2,128]{2,1,0:T(2,128)S(1)}, u32[]{:S(2)}, u32[]{:S(2)}) collective-permute-start(f32[4,2,128]{2,1,0:T(2,128)S(1)} %get-tuple-element.156), channel_id=1, source_target_pairs={{16,0},{32,16},{48,32},{64,48},{80,64},{96,80},{112,96},{128,112},... | collective-permute-start | bytes 12296 | tf_op jit(solution)/shard_map/ppermute | solution.py:31
  375.8 7.2 %collective-permute-start.30 = (f32[4,68,2]{2,1,0:T(8,128)S(1)}, f32[4,68,2]{2,1,0:T(8,128)S(1)}, u32[]{:S(2)}, u32[]{:S(2)}) collective-permute-start(f32[4,68,2]{2,1,0:T(8,128)S(1)} %get-tuple-element.137), channel_id=1, source_target_pairs={{0,1},{1,2},{2,3},{3,4},{4,5},{5,6},{6,7},{7,8},{8,9},{9,10},{10,1... | collective-permute-start | bytes 6536 | tf_op jit(solution)/shard_map/ppermute | solution.py:29
  379.7 6.5 %collective-permute-start.31 = (f32[4,68,2]{2,1,0:T(8,128)S(1)}, f32[4,68,2]{2,1,0:T(8,128)S(1)}, u32[]{:S(2)}, u32[]{:S(2)}) collective-permute-start(f32[4,68,2]{2,1,0:T(8,128)S(1)} %get-tuple-element.138), channel_id=1, source_target_pairs={{1,0},{2,1},{3,2},{4,3},{5,4},{6,5},{7,6},{8,7},{9,8},{10,9},{11,1... | collective-permute-start | bytes 6536 | tf_op jit(solution)/shard_map/ppermute | solution.py:31
  402.9 12.0 %all-to-all-start.11 = ((f32[16,1,256]{2,1,0:T(1,128)}), f32[16,1,256]{2,1,0:T(1,128)S(1)}, u32[]{:S(2)}, u32[]{:S(2)}) async-start(f32[16,1,256]{2,1,0:T(1,128)} %all_to_all.76), calls=%async_computation.11 | async-start | bytes 32768 | tf_op jit(solution)/shard_map/all_to_all | solution.py:129
  416.9 9.5 %all-to-all-start.12 = ((f32[16,1,256]{2,1,0:T(1,128)}), f32[16,1,256]{2,1,0:T(1,128)S(1)}, u32[]{:S(2)}, u32[]{:S(2)}) async-start(f32[16,1,256]{2,1,0:T(1,128)} %mul.479), calls=%async_computation.12 | async-start | bytes 32768 | tf_op jit(solution)/shard_map/all_to_all | solution.py:140
  (12 other events, 42.0 us)
